TPU v7x, 32 devices: a whole 2x2x4 slice. The times are simulated.
32 devices in a mesh: groups: 2 (over y), ep: 4 (over z), sub: 2 (over x), tp: 2 (over core).
Axes of the slice: x: 2, y: 2, z: 4, core: 2. Of those that a mesh axis runs over, the one named last changes fastest.
Arguments:
- rows: bfloat16 [1024, 4096], P(('groups', 'ep'), ('sub', 'tp')), parts along dimension 0, may hold values from -6 to 6
- path: int32 [4, 1024, 1], P(None, ('groups', 'ep')), parts along dimension 1, may hold values from 0 to 7; in each aligned block of 128 rows (0 to 127, 128 to 255, ..., all dimensions but the last counted through in order) at most 32 rows name the same one
- norm_gain: float32 [8, 4096], P(('ep', 'tp')), may hold values from 0.1 to 1.9
- gate_weight: bfloat16 [8, 1408, 4096], P(('ep', 'tp'), 'sub'), may hold values from -0.09375 to 0.09375
- up_weight: bfloat16 [8, 1408, 4096], P(('ep', 'tp'), 'sub'), may hold values from -0.09375 to 0.09375
- down_weight: bfloat16 [8, 1408, 4096], P(('ep', 'tp'), 'sub'), may hold values from -0.15625 to 0.15625
Outputs:
- chained: bfloat16 [1024, 4096], P(('groups', 'ep'), ('sub', 'tp')), parts along dimension 0
There are 2 independent parts, one for each index of `groups`. A program takes and returns all parts, laid end to end along the dimension named above; an argument that names none is the same for every part. Nothing has to cross between parts.
Inputs may be any that keep to these rules, and one draw needn't show every extreme that they name: `path`: in each aligned block of 128 rows of one hop no expert is named by more than 32 rows, and in some blocks one expert is named by exactly 32.
All inputs are finite; a program needn't handle non-finite values.
Results may differ from a plain program's by a relative error of at most 0.02.
Values may be sent and summed in bfloat16 or wider, within the bound.
A program may use at most 64 MiB of HBM per device.

v0:
```python
import jax
import jax.numpy as jnp
from jax import lax
from jax.sharding import PartitionSpec as P

EPS = 1e-06


def slot_table(routing, experts, per_pair, core_count, core_index, capacity):
    onehot = (routing[:, None] == jnp.arange(experts, dtype=jnp.int32)[None, :]).astype(jnp.int32)
    before = jnp.cumsum(onehot, axis=0) - onehot
    rank_in = jnp.sum(before * onehot, axis=1)
    pair_index = routing // per_pair
    owner_core = pair_index % core_count
    dest_index = pair_index // core_count
    local_index = routing % per_pair
    target = (dest_index * per_pair + local_index) * capacity + rank_in
    target = jnp.where(owner_core == core_index, target, -1)
    slot_count = experts // core_count * capacity
    slots = jnp.arange(slot_count, dtype=jnp.int32)
    return (slots[:, None] == target[None, :]).astype(jnp.bfloat16)


def expert_update(inputs, gains, gate_weight, up_weight, down_weight):
    values = inputs.astype(jnp.float32)
    meansq = jnp.mean(values * values, axis=-1, keepdims=True)
    normed = (values * lax.rsqrt(meansq + EPS) * gains[None, :, None, :]).astype(jnp.bfloat16)
    gate = jnp.einsum("slcd,lhd->slch", normed, gate_weight, preferred_element_type=jnp.float32)
    upward = jnp.einsum("slcd,lhd->slch", normed, up_weight, preferred_element_type=jnp.float32)
    hidden = (jax.nn.silu(gate) * upward).astype(jnp.bfloat16)
    partial_value = jnp.einsum(
        "slch,lhd->slcd", hidden, down_weight, preferred_element_type=jnp.float32
    )
    return partial_value.astype(jnp.bfloat16)


def shards(rows, path, norm_gain, gate_weight, up_weight, down_weight):
    local_rows = rows.shape[0]
    per_pair = gate_weight.shape[0]
    ep_count = lax.axis_size("ep")
    core_count = lax.axis_size("tp")
    core_index = lax.axis_index("tp")
    experts = ep_count * core_count * per_pair
    capacity = 2 * local_rows // experts
    state = rows
    for hop_index in range(path.shape[0]):
        placing = slot_table(
            path[hop_index, :, 0], experts, per_pair, core_count, core_index, capacity
        )
        whole = lax.all_gather(state, ("sub", "tp"), axis=1, tiled=True)
        packed = jnp.dot(placing, whole, preferred_element_type=jnp.float32).astype(jnp.bfloat16)
        packed = packed.reshape(ep_count, per_pair, capacity, whole.shape[1])
        arrived = lax.all_to_all(packed, "ep", split_axis=0, concat_axis=0, tiled=True)
        partial_value = expert_update(arrived, norm_gain, gate_weight, up_weight, down_weight)
        summed = (
            lax.psum_scatter(partial_value, "sub", scatter_dimension=3, tiled=True)
            .astype(jnp.float32)
            .astype(jnp.bfloat16)
        )
        returned = lax.all_to_all(summed, "ep", split_axis=0, concat_axis=0, tiled=True)
        flat_back = returned.reshape(ep_count * per_pair * capacity, returned.shape[3])
        per_row = jnp.einsum("sr,sd->rd", placing, flat_back, preferred_element_type=jnp.float32)
        update = lax.psum_scatter(
            per_row.astype(jnp.bfloat16), "tp", scatter_dimension=1, tiled=True
        )
        update = lax.optimization_barrier(update)
        state = (state.astype(jnp.float32) + update.astype(jnp.float32)).astype(jnp.bfloat16)
    return state


def solution(mesh):
    in_specs = (
        P(("groups", "ep"), ("sub", "tp")),
        P(None, ("groups", "ep"), None),
        P(("ep", "tp"), None),
        P(("ep", "tp"), "sub", None),
        P(("ep", "tp"), "sub", None),
        P(("ep", "tp"), "sub", None),
    )
    out_specs = P(("groups", "ep"), ("sub", "tp"))
    return jax.shard_map(shards, mesh=mesh, in_specs=in_specs, out_specs=out_specs, check_vma=False)
```

profile of v0, /device:TPU:1, one launch (start us, length us, event | category | flops | bytes accessed | tf_op | source)
XLA Modules:
  0.0 460.9 jit_solution(9528648651488733435)
XLA Ops:
  10.2 18.0 %all-gather.5.cloned.1.call-done = bf16[128,4096]{1,0:T(8,128)(2,1)} async-done(((bf16[128,1024]{1,0:T(8,128)(2,1)}), bf16[128,4096]{1,0:T(8,128)(2,1)}) %all-gather.5.cloned.1.call-update) | async-done | bytes 1048592 | tf_op jit(solution)/shard_map/all_gather | solution.py:50
  29.8 29.4 %all_to_all.40 = bf16[4,1,32,4096]{3,2,1,0:T(8,128)(2,1)S(1)} all-to-all(bf16[4,1,32,4096]{3,2,1,0:T(8,128)(2,1)S(1)} %bitcast.283), channel_id=1, replica_groups=mesh['groups'=2,'ep'=4,'sub'=2,'tp'=2] {'ep'}, dimensions={0} | all-to-all | bytes 2097152 | tf_op jit(solution)/shard_map/all_to_all | solution.py:53
  64.1 9.0 %fusion.45 = bf16[4,1,32,4096]{3,2,0,1:T(8,128)(2,1)} fusion(bf16[1,704,4096]{2,1,0:T(8,128)(2,1)} %param.11, bf16[1,704,4096]{2,1,0:T(8,128)(2,1)} %param.10, bf16[4,1,32,4096]{3,2,1,0:T(8,128)(2,1)S(1)} %all_to_all.40, f32[4096]{0:T(1024)S(1)} %bitcast.296, f32[4,32]{1,0:T(4,128)S(1)} %add_rsqrt_fusion.3, f32[4,1,32,704]{3,2,0,1:T(8,128)S(1)} %fusion.60), kind=kOutput, calls=%fused_computation.35 | convolution fusion | flops 1479557120 | bytes 14008832 | tf_op jit(solution)/shard_map/slch,lhd->slcd/dot_general | solution.py:31
  73.2 19.3 %reduce-scatter.9.cloned.1.call-done = bf16[4,1,32,2048]{3,2,0,1:T(8,128)(2,1)} async-done(((bf16[4,1,32,4096]{3,2,0,1:T(8,128)(2,1)}), bf16[4,1,32,2048]{3,2,0,1:T(8,128)(2,1)}) %reduce-scatter.9.cloned.1.call-update) | async-done | bytes 524304 | tf_op jit(solution)/shard_map/reduce_scatter | solution.py:56
  92.5 18.0 %all_to_all.41 = bf16[4,1,32,2048]{3,2,1,0:T(8,128)(2,1)S(1)} all-to-all(bf16[4,1,32,2048]{3,2,1,0:T(8,128)(2,1)} %bitcast.291), channel_id=1, replica_groups=mesh['groups'=2,'ep'=4,'sub'=2,'tp'=2] {'ep'}, dimensions={0} | all-to-all | bytes 1048576 | tf_op jit(solution)/shard_map/all_to_all | solution.py:60
  111.7 7.7 %reduce-scatter.11.cloned.1.call-done = bf16[128,1024]{1,0:T(8,128)(2,1)} async-done(((bf16[128,2048]{1,0:T(8,128)(2,1)}), bf16[128,1024]{1,0:T(8,128)(2,1)}) %reduce-scatter.11.cloned.1.call-update) | async-done | bytes 262160 | tf_op jit(solution)/shard_map/reduce_scatter | solution.py:63
  121.1 18.0 %all-gather.7.cloned.1.call-done = bf16[128,4096]{1,0:T(8,128)(2,1)} async-done(((bf16[128,1024]{1,0:T(8,128)(2,1)}), bf16[128,4096]{1,0:T(8,128)(2,1)}) %all-gather.7.cloned.1.call-update) | async-done | bytes 1048592 | tf_op jit(solution)/shard_map/all_gather | solution.py:50
  140.8 29.4 %all_to_all.42 = bf16[4,1,32,4096]{3,2,1,0:T(8,128)(2,1)S(1)} all-to-all(bf16[4,1,32,4096]{3,2,1,0:T(8,128)(2,1)S(1)} %bitcast.284), channel_id=1, replica_groups=mesh['groups'=2,'ep'=4,'sub'=2,'tp'=2] {'ep'}, dimensions={0} | all-to-all | bytes 2097152 | tf_op jit(solution)/shard_map/all_to_all | solution.py:53
  175.2 9.0 %fusion.42 = bf16[4,1,32,4096]{3,2,0,1:T(8,128)(2,1)} fusion(bf16[1,704,4096]{2,1,0:T(8,128)(2,1)} %param.11, bf16[1,704,4096]{2,1,0:T(8,128)(2,1)} %param.10, bf16[4,1,32,4096]{3,2,1,0:T(8,128)(2,1)S(1)} %all_to_all.42, f32[4,32]{1,0:T(4,128)S(1)} %add_rsqrt_fusion.2, f32[4096]{0:T(1024)S(1)} %bitcast.298, f32[4,1,32,704]{3,2,0,1:T(8,128)S(1)} %fusion.63), kind=kOutput, calls=%fused_computation.34 | convolution fusion | flops 1479557120 | bytes 14008832 | tf_op jit(solution)/shard_map/slch,lhd->slcd/dot_general | solution.py:31
  184.2 19.3 %reduce-scatter.13.cloned.1.call-done = bf16[4,1,32,2048]{3,2,0,1:T(8,128)(2,1)} async-done(((bf16[4,1,32,4096]{3,2,0,1:T(8,128)(2,1)}), bf16[4,1,32,2048]{3,2,0,1:T(8,128)(2,1)}) %reduce-scatter.13.cloned.1.call-update) | async-done | bytes 524304 | tf_op jit(solution)/shard_map/reduce_scatter | solution.py:56
  203.5 18.0 %all_to_all.43 = bf16[4,1,32,2048]{3,2,1,0:T(8,128)(2,1)S(1)} all-to-all(bf16[4,1,32,2048]{3,2,1,0:T(8,128)(2,1)} %bitcast.292), channel_id=1, replica_groups=mesh['groups'=2,'ep'=4,'sub'=2,'tp'=2] {'ep'}, dimensions={0} | all-to-all | bytes 1048576 | tf_op jit(solution)/shard_map/all_to_all | solution.py:60
  222.9 7.5 %reduce-scatter.15.cloned.1.call-done = bf16[128,1024]{1,0:T(8,128)(2,1)} async-done(((bf16[128,2048]{1,0:T(8,128)(2,1)}), bf16[128,1024]{1,0:T(8,128)(2,1)}) %reduce-scatter.15.cloned.1.call-update) | async-done | bytes 262160 | tf_op jit(solution)/shard_map/reduce_scatter | solution.py:63
  232.2 18.0 %all-gather.9.cloned.1.call-done = bf16[128,4096]{1,0:T(8,128)(2,1)} async-done(((bf16[128,1024]{1,0:T(8,128)(2,1)}), bf16[128,4096]{1,0:T(8,128)(2,1)}) %all-gather.9.cloned.1.call-update) | async-done | bytes 1048592 | tf_op jit(solution)/shard_map/all_gather | solution.py:50
  251.9 29.4 %all_to_all.44 = bf16[4,1,32,4096]{3,2,1,0:T(8,128)(2,1)S(1)} all-to-all(bf16[4,1,32,4096]{3,2,1,0:T(8,128)(2,1)S(1)} %bitcast.285), channel_id=1, replica_groups=mesh['groups'=2,'ep'=4,'sub'=2,'tp'=2] {'ep'}, dimensions={0} | all-to-all | bytes 2097152 | tf_op jit(solution)/shard_map/all_to_all | solution.py:53
  286.2 9.0 %fusion.39 = bf16[4,1,32,4096]{3,2,0,1:T(8,128)(2,1)} fusion(bf16[1,704,4096]{2,1,0:T(8,128)(2,1)} %param.11, bf16[1,704,4096]{2,1,0:T(8,128)(2,1)} %param.10, bf16[4,1,32,4096]{3,2,1,0:T(8,128)(2,1)S(1)} %all_to_all.44, f32[4,32]{1,0:T(4,128)S(1)} %add_rsqrt_fusion.1, f32[4096]{0:T(1024)S(1)} %bitcast.300, f32[4,1,32,704]{3,2,0,1:T(8,128)S(1)} %fusion.66), kind=kOutput, calls=%fused_computation.33 | convolution fusion | flops 1479557120 | bytes 14008832 | tf_op jit(solution)/shard_map/slch,lhd->slcd/dot_general | solution.py:31
  295.3 19.2 %reduce-scatter.17.cloned.1.call-done = bf16[4,1,32,2048]{3,2,0,1:T(8,128)(2,1)} async-done(((bf16[4,1,32,4096]{3,2,0,1:T(8,128)(2,1)}), bf16[4,1,32,2048]{3,2,0,1:T(8,128)(2,1)}) %reduce-scatter.17.cloned.1.call-update) | async-done | bytes 524304 | tf_op jit(solution)/shard_map/reduce_scatter | solution.py:56
  314.5 18.0 %all_to_all.45 = bf16[4,1,32,2048]{3,2,1,0:T(8,128)(2,1)S(1)} all-to-all(bf16[4,1,32,2048]{3,2,1,0:T(8,128)(2,1)} %bitcast.293), channel_id=1, replica_groups=mesh['groups'=2,'ep'=4,'sub'=2,'tp'=2] {'ep'}, dimensions={0} | all-to-all | bytes 1048576 | tf_op jit(solution)/shard_map/all_to_all | solution.py:60
  333.7 7.7 %reduce-scatter.19.cloned.1.call-done = bf16[128,1024]{1,0:T(8,128)(2,1)} async-done(((bf16[128,2048]{1,0:T(8,128)(2,1)}), bf16[128,1024]{1,0:T(8,128)(2,1)}) %reduce-scatter.19.cloned.1.call-update) | async-done | bytes 262160 | tf_op jit(solution)/shard_map/reduce_scatter | solution.py:63
  343.2 18.0 %all-gather.11.cloned.1.call-done = bf16[128,4096]{1,0:T(8,128)(2,1)} async-done(((bf16[128,1024]{1,0:T(8,128)(2,1)}), bf16[128,4096]{1,0:T(8,128)(2,1)}) %all-gather.11.cloned.1.call-update) | async-done | bytes 1048592 | tf_op jit(solution)/shard_map/all_gather | solution.py:50
  362.9 29.4 %all_to_all.46 = bf16[4,1,32,4096]{3,2,1,0:T(8,128)(2,1)S(1)} all-to-all(bf16[4,1,32,4096]{3,2,1,0:T(8,128)(2,1)S(1)} %bitcast.286), channel_id=1, replica_groups=mesh['groups'=2,'ep'=4,'sub'=2,'tp'=2] {'ep'}, dimensions={0} | all-to-all | bytes 2097152 | tf_op jit(solution)/shard_map/all_to_all | solution.py:53
  397.2 9.0 %fusion.36 = bf16[4,1,32,4096]{3,2,0,1:T(8,128)(2,1)} fusion(bf16[1,704,4096]{2,1,0:T(8,128)(2,1)} %param.11, bf16[1,704,4096]{2,1,0:T(8,128)(2,1)} %param.10, bf16[4,1,32,4096]{3,2,1,0:T(8,128)(2,1)S(1)} %all_to_all.46, f32[4,32]{1,0:T(4,128)S(1)} %add_rsqrt_fusion, f32[4096]{0:T(1024)S(1)} %bitcast.302, f32[4,1,32,704]{3,2,0,1:T(8,128)S(1)} %fusion.69), kind=kOutput, calls=%fused_computation.32 | convolution fusion | flops 1479557120 | bytes 14008832 | tf_op jit(solution)/shard_map/slch,lhd->slcd/dot_general | solution.py:31
  406.3 19.2 %reduce-scatter.21.cloned.1.call-done = bf16[4,1,32,2048]{3,2,0,1:T(8,128)(2,1)} async-done(((bf16[4,1,32,4096]{3,2,0,1:T(8,128)(2,1)}), bf16[4,1,32,2048]{3,2,0,1:T(8,128)(2,1)}) %reduce-scatter.21.cloned.1.call-update) | async-done | bytes 524304 | tf_op jit(solution)/shard_map/reduce_scatter | solution.py:56
  425.5 18.0 %all_to_all.47 = bf16[4,1,32,2048]{3,2,1,0:T(8,128)(2,1)S(1)} all-to-all(bf16[4,1,32,2048]{3,2,1,0:T(8,128)(2,1)} %bitcast.294), channel_id=1, replica_groups=mesh['groups'=2,'ep'=4,'sub'=2,'tp'=2] {'ep'}, dimensions={0} | all-to-all | bytes 1048576 | tf_op jit(solution)/shard_map/all_to_all | solution.py:60
  444.6 7.7 %reduce-scatter.23.cloned.1.call-done = bf16[128,1024]{1,0:T(8,128)(2,1)} async-done(((bf16[128,2048]{1,0:T(8,128)(2,1)}), bf16[128,1024]{1,0:T(8,128)(2,1)}) %reduce-scatter.23.cloned.1.call-update) | async-done | bytes 262160 | tf_op jit(solution)/shard_map/reduce_scatter | solution.py:63
  (70 shorter events, 41.9 us)
Async XLA Ops:
  6.5 21.6 %all-gather.5.cloned.1.call-start = ((), (), s32[]{:S(2)}) async-start(), calls=%async_computation.16 | async-start | bytes 1310720 | tf_op jit(solution)/shard_map/all_gather | solution.py:50
  7.3 85.2 %reduce-scatter.9.cloned.1.call-start = ((), (), s32[]{:S(2)}) async-start(), calls=%async_computation.17 | async-start | bytes 1572864 | tf_op jit(solution)/shard_map/reduce_scatter | solution.py:56
  29.8 29.7 %copy-start.4 = (f32[1,4096]{1,0:T(1,128)S(1)}, f32[1,4096]{1,0:T(1,128)}, u32[]{:S(2)}) copy-start(f32[1,4096]{1,0:T(1,128)} %param.8) | copy-start | bytes 49156
  73.1 46.2 %copy-start.3 = (bf16[128,1024]{1,0:T(8,128)(2,1)S(1)}, bf16[128,1024]{1,0:T(8,128)(2,1)}, u32[]{:S(2)}) copy-start(bf16[128,1024]{1,0:T(8,128)(2,1)} %param.6) | copy-start | bytes 786436
  73.2 46.2 %reduce-scatter.11.cloned.1.call-start = ((), (), s32[]{:S(2)}) async-start(), calls=%async_computation.18 | async-start | bytes 786432 | tf_op jit(solution)/shard_map/reduce_scatter | solution.py:63
  111.6 27.6 %all-gather.7.cloned.1.call-start = ((), (), s32[]{:S(2)}) async-start(), calls=%async_computation.19 | async-start | bytes 1310720 | tf_op jit(solution)/shard_map/all_gather | solution.py:50
  121.1 82.4 %reduce-scatter.13.cloned.1.call-start = ((), (), s32[]{:S(2)}) async-start(), calls=%async_computation.20 | async-start | bytes 1572864 | tf_op jit(solution)/shard_map/reduce_scatter | solution.py:56
  184.2 46.2 %copy-start.1 = (bf16[128,1024]{1,0:T(8,128)(2,1)S(1)}, bf16[128,1024]{1,0:T(8,128)(2,1)}, u32[]{:S(2)}) copy-start(bf16[128,1024]{1,0:T(8,128)(2,1)} %add_convert_fusion.3) | copy-start | bytes 786436
  184.2 46.2 %reduce-scatter.15.cloned.1.call-start = ((), (), s32[]{:S(2)}) async-start(), calls=%async_computation.21 | async-start | bytes 786432 | tf_op jit(solution)/shard_map/reduce_scatter | solution.py:63
  222.6 27.6 %all-gather.9.cloned.1.call-start = ((), (), s32[]{:S(2)}) async-start(), calls=%async_computation.22 | async-start | bytes 1310720 | tf_op jit(solution)/shard_map/all_gather | solution.py:50
  232.1 82.4 %reduce-scatter.17.cloned.1.call-start = ((), (), s32[]{:S(2)}) async-start(), calls=%async_computation.23 | async-start | bytes 1572864 | tf_op jit(solution)/shard_map/reduce_scatter | solution.py:56
  295.2 46.2 %copy-start = (bf16[128,1024]{1,0:T(8,128)(2,1)S(1)}, bf16[128,1024]{1,0:T(8,128)(2,1)}, u32[]{:S(2)}) copy-start(bf16[128,1024]{1,0:T(8,128)(2,1)} %add_convert_fusion.2) | copy-start | bytes 786436
  295.2 46.1 %reduce-scatter.19.cloned.1.call-start = ((), (), s32[]{:S(2)}) async-start(), calls=%async_computation.24 | async-start | bytes 786432 | tf_op jit(solution)/shard_map/reduce_scatter | solution.py:63
  333.7 27.5 %all-gather.11.cloned.1.call-start = ((), (), s32[]{:S(2)}) async-start(), calls=%async_computation.25 | async-start | bytes 1310720 | tf_op jit(solution)/shard_map/all_gather | solution.py:50
  343.1 82.4 %reduce-scatter.21.cloned.1.call-start = ((), (), s32[]{:S(2)}) async-start(), calls=%async_computation.26 | async-start | bytes 1572864 | tf_op jit(solution)/shard_map/reduce_scatter | solution.py:56
  406.2 46.2 %copy-start.2 = (bf16[128,1024]{1,0:T(8,128)(2,1)S(1)}, bf16[128,1024]{1,0:T(8,128)(2,1)}, u32[]{:S(2)}) copy-start(bf16[128,1024]{1,0:T(8,128)(2,1)} %add_convert_fusion.1) | copy-start | bytes 786436
  406.2 46.2 %reduce-scatter.23.cloned.1.call-start = ((), (), s32[]{:S(2)}) async-start(), calls=%async_computation.27 | async-start | bytes 786432 | tf_op jit(solution)/shard_map/reduce_scatter | solution.py:63
Sparse Core Ops, SparseCore 0:
  8.9 19.1 all-gather.4
  73.3 19.1 reduce-scatter.8
  111.7 7.5 reduce-scatter.10
  121.2 17.9 all-gather.6
  184.3 19.1 reduce-scatter.12
  222.8 7.5 reduce-scatter.14
  232.2 17.9 all-gather.8
  295.3 19.1 reduce-scatter.16
  333.8 7.5 reduce-scatter.18
  343.2 17.9 all-gather.10
  406.3 19.1 reduce-scatter.20
  444.8 7.5 reduce-scatter.22
where the time goes:
time: 462 us; the launch traced here: 461 us
  blocking collectives  190 us (41%)
  waiting for transfers between devices  181 us (39%)
  matrix products  65.5 us (14%)
  between operations  13.7 us (3%)
  other arithmetic  10.2 us (2%)
    all_to_all x4, blocking collectives, shards(): lax.all_to_all(packed, 'ep', split_axis=0, concat_axis=0, tiled=True)  118 us
    reduce_scatter x4, waiting for transfers between devices, shards(): lax.psum_scatter(partial_value, 'sub', scatter_dimension=3, tiled=True)  77.1 us
    all_gather x4, waiting for transfers between devices, shards(): whole = lax.all_gather(state, ('sub', 'tp'), axis=1, tiled=True)  72.1 us
    all_to_all x4, blocking collectives, shards(): lax.all_to_all(summed, 'ep', split_axis=0, concat_axis=0, tiled=True)  71.9 us
    dot_general x4, matrix products, expert_update(): jnp.einsum('slch,lhd->slcd', hidden, down_weight, preferred_element_type=...  36.1 us
    reduce_scatter x4, waiting for transfers between devices, shards(): lax.psum_scatter(per_row.astype(jnp.bfloat16), 'tp', scatter_dimension=1,...  30.6 us
    dot_general x4, matrix products, expert_update(): jnp.einsum('slcd,lhd->slch', normed, gate_weight, preferred_element_type=...  18.3 us
  transfers between devices with their start and end apart: 12, of which 12 were waited for; matrix products, arithmetic and copies ran while one was open for 1% of the time, Pallas kernels for 0%

commit v1 on v0

v1 whole, which is shorter than its diff:
```python
import functools

import jax
import jax.numpy as jnp
from jax import lax
from jax.experimental import pallas as pl
from jax.experimental.pallas import tpu as pltpu
from jax.sharding import PartitionSpec as P

EPS = 1e-06
MESH = pl.DeviceIdType.MESH
F32 = jnp.float32
BF16 = jnp.bfloat16


def partner(index, distance, count):
    out, bit = 0, 1
    while bit < count:
        own = (index // bit) % 2
        out = out + bit * ((1 - own) if (distance // bit) % 2 else own)
        bit *= 2
    return out


def chain_kernel(
    sizes,
    rows_ref,
    path_ref,
    gain_ref,
    gate_hbm,
    up_hbm,
    down_hbm,
    state_ref,
    gate_ref,
    up_ref,
    down_ref,
    placing_ref,
    packed_ref,
    arrived_ref,
    normed_ref,
    hidden_ref,
    part_out_ref,
    part_in_ref,
    own_ref,
    summed_ref,
    returned_ref,
    load_sem,
    disp_send,
    disp_recv,
    fwd_send,
    fwd_recv,
    part_send,
    part_recv,
    ret_send,
    ret_recv,
):
    ep, tp, sub, cap, per_chunk = sizes
    z, s, t = lax.axis_index("ep"), lax.axis_index("sub"), lax.axis_index("tp")
    hops = path_ref.shape[0]
    local_rows, quarter = state_ref.shape
    half = quarter * tp
    experts = ep * tp
    chunks = ep // per_chunk
    chunk_rows = per_chunk * cap
    here = s * tp + t

    loads = [
        pltpu.make_async_copy(src, dst, load_sem.at[i])
        for i, (src, dst) in enumerate(
            ((gate_hbm, gate_ref), (up_hbm, up_ref), (down_hbm, down_ref))
        )
    ]
    for load in loads:
        load.start()

    barrier = pltpu.get_barrier_semaphore()
    peers = 0
    for k in range(ep):
        for c in range(tp):
            if k or c:
                pl.semaphore_signal(
                    barrier, inc=1,
                    device_id={"ep": partner(z, k, ep), "tp": (t + c) % tp},
                    device_id_type=MESH,
                )
                peers += 1
    for j in range(1, sub):
        pl.semaphore_signal(
            barrier, inc=1, device_id={"sub": (s + j) % sub}, device_id_type=MESH
        )
        peers += 1

    def rows_of(k):
        return pl.ds(k * cap, cap)

    def rows_in(chunk):
        return pl.ds(chunk * chunk_rows, chunk_rows)

    def dispatch_copy(k, c):
        to_z, to_t = partner(z, k, ep), (t + c) % tp
        return pltpu.make_async_remote_copy(
            src_ref=packed_ref.at[to_z * tp + to_t],
            dst_ref=arrived_ref.at[here, rows_of(k)],
            send_sem=disp_send.at[k, c],
            recv_sem=disp_recv.at[k, c],
            device_id={"ep": to_z, "tp": to_t},
            device_id_type=MESH,
        )

    def forward_copy(k, j):
        block = arrived_ref.at[pl.ds(s * tp, tp), rows_of(k)]
        return pltpu.make_async_remote_copy(
            src_ref=block,
            dst_ref=block,
            send_sem=fwd_send.at[k, j - 1],
            recv_sem=fwd_recv.at[k, j - 1],
            device_id={"sub": (s + j) % sub},
            device_id_type=MESH,
        )

    def part_copy(chunk, j):
        return pltpu.make_async_remote_copy(
            src_ref=part_out_ref.at[j - 1, rows_in(chunk)],
            dst_ref=part_in_ref.at[j - 1, rows_in(chunk)],
            send_sem=part_send.at[chunk, j - 1],
            recv_sem=part_recv.at[chunk, j - 1],
            device_id={"sub": (s + j) % sub},
            device_id_type=MESH,
        )

    def return_copy(k, c):
        to_z, to_t = partner(z, k, ep), (t + c) % tp
        return pltpu.make_async_remote_copy(
            src_ref=summed_ref.at[to_t, rows_of(k)],
            dst_ref=returned_ref.at[z * tp + t],
            send_sem=ret_send.at[k, c],
            recv_sem=ret_recv.at[k, c],
            device_id={"ep": to_z, "tp": to_t},
            device_id_type=MESH,
        )

    remote = [(k, c) for k in range(ep) for c in range(tp) if k or c]

    def make_placing(hop):
        named = path_ref[pl.ds(hop, 1), :]
        lines = -(-experts // 8) * 8
        onehot = (
            lax.broadcasted_iota(jnp.int32, (lines, local_rows), 0) == named
        ).astype(F32)
        earlier = (
            lax.broadcasted_iota(jnp.int32, (local_rows, local_rows), 0)
            < lax.broadcasted_iota(jnp.int32, (local_rows, local_rows), 1)
        ).astype(F32)
        before = jnp.dot(
            onehot.astype(BF16), earlier.astype(BF16), preferred_element_type=F32
        )
        rank = jnp.sum(before * onehot, axis=0, keepdims=True)
        target = named.astype(F32) * float(cap) + rank
        slots = lax.broadcasted_iota(jnp.int32, (experts * cap, local_rows), 0)
        placing_ref[hop] = jnp.where(slots.astype(F32) == target, 1.0, 0.0).astype(BF16)

    def dispatch(hop):
        packed = jnp.dot(
            placing_ref[hop], state_ref[...], preferred_element_type=F32
        ).astype(BF16)
        packed_ref[...] = packed.reshape(experts, cap, quarter)
        for k, c in remote:
            dispatch_copy(k, c).start()
        arrived_ref[here, rows_of(0), :] = packed_ref[z * tp + t]

    def forward(k):
        for c in range(tp):
            if k or c:
                dispatch_copy(k, c).wait_recv()
        for j in range(1, sub):
            forward_copy(k, j).start()

    def normalise(k):
        for j in range(1, sub):
            forward_copy(k, j).wait_recv()
        total = jnp.zeros((cap, 1), F32)
        for q in range(sub * tp):
            value = arrived_ref[q, rows_of(k), :].astype(F32)
            total = total + jnp.sum(value * value, axis=-1, keepdims=True)
        scale = lax.rsqrt(total / float(quarter * sub * tp) + EPS)
        for q in range(sub * tp):
            value = arrived_ref[q, rows_of(k), :].astype(F32)
            columns = pl.ds(q * quarter, quarter)
            normed_ref[rows_of(k), columns] = (
                value * scale * gain_ref[:, columns]
            ).astype(BF16)

    def expand(chunk):
        for k in range(chunk * per_chunk, (chunk + 1) * per_chunk):
            normalise(k)
        normed = normed_ref[rows_in(chunk), :]
        dims = (((1,), (1,)), ((), ()))
        gate = lax.dot_general(normed, gate_ref[0], dims, preferred_element_type=F32)
        upward = lax.dot_general(normed, up_ref[0], dims, preferred_element_type=F32)
        hidden_ref[rows_in(chunk), :] = (
            gate / (1.0 + jnp.exp(-gate)) * upward
        ).astype(BF16)

    tile = min(512, half)

    def contract(chunk, j, out):
        base = ((s + j) % sub) * half

        def step(i, carry):
            inside = pl.ds(pl.multiple_of(i * tile, tile), tile)
            columns = pl.ds(pl.multiple_of(base + i * tile, tile), tile)
            out[rows_in(chunk), inside] = jnp.dot(
                hidden_ref[rows_in(chunk), :],
                down_ref[0, :, columns],
                preferred_element_type=F32,
            ).astype(out.dtype)
            return carry

        lax.fori_loop(0, half // tile, step, 0)

    def project(chunk):
        for j in range(1, sub):
            contract(chunk, j, part_out_ref.at[j - 1])
            part_copy(chunk, j).start()
        contract(chunk, 0, own_ref)

    def give_back(chunk):
        for j in range(1, sub):
            part_copy(chunk, j).wait_recv()
        for k in range(chunk * per_chunk, (chunk + 1) * per_chunk):
            for i in range(tp):
                columns = pl.ds(i * quarter, quarter)
                value = own_ref[rows_of(k), columns]
                for j in range(1, sub):
                    value = value + part_in_ref[j - 1, rows_of(k), columns].astype(F32)
                summed_ref[i, rows_of(k), :] = value.astype(BF16)
            for c in range(tp):
                if k or c:
                    return_copy(k, c).start()
                else:
                    returned_ref[z * tp + t] = summed_ref[t, rows_of(k), :]

    state_ref[...] = rows_ref[...]
    make_placing(0)
    pl.semaphore_wait(barrier, peers)
    dispatch(0)
    for hop in range(1, hops):
        make_placing(hop)
    for load in loads:
        load.wait()

    def one_hop(hop, carry):
        for k in range(per_chunk):
            forward(k)
        expand(0)
        for k in range(per_chunk, ep):
            forward(k)
        project(0)
        for chunk in range(1, chunks):
            expand(chunk)
            project(chunk)
        for k, c in remote:
            dispatch_copy(k, c).wait_send()
        for k in range(ep):
            for j in range(1, sub):
                forward_copy(k, j).wait_send()
        for chunk in range(chunks):
            give_back(chunk)
        for chunk in range(chunks):
            for j in range(1, sub):
                part_copy(chunk, j).wait_send()
        for k, c in remote:
            return_copy(k, c).wait_recv()
        update = lax.dot_general(
            placing_ref[hop],
            returned_ref[...].reshape(experts * cap, quarter),
            (((0,), (0,)), ((), ())),
            preferred_element_type=F32,
        )
        state_ref[...] = (state_ref[...].astype(F32) + update).astype(BF16)

        @pl.when(hop < hops - 1)
        def _():
            dispatch(hop + 1)

        for k, c in remote:
            return_copy(k, c).wait_send()
        return carry

    lax.fori_loop(0, hops, one_hop, 0)


def shards(sizes, rows, path, norm_gain, gate_weight, up_weight, down_weight):
    ep, tp, sub, cap, per_chunk = sizes
    local_rows, quarter = rows.shape
    hops = path.shape[0]
    hid, width = gate_weight.shape[1:]
    half = quarter * tp
    experts = ep * tp
    chunks = ep // per_chunk
    dma = pltpu.SemaphoreType.DMA
    vmem, any_space = pl.BlockSpec(memory_space=pltpu.VMEM), pl.BlockSpec(memory_space=pl.ANY)
    return pl.pallas_call(
        functools.partial(chain_kernel, sizes),
        out_shape=jax.ShapeDtypeStruct(rows.shape, rows.dtype),
        in_specs=[vmem, vmem, vmem, any_space, any_space, any_space],
        out_specs=vmem,
        scratch_shapes=[
            pltpu.VMEM((1, hid, width), BF16),
            pltpu.VMEM((1, hid, width), BF16),
            pltpu.VMEM((1, hid, width), BF16),
            pltpu.VMEM((hops, experts * cap, local_rows), BF16),
            pltpu.VMEM((experts, cap, quarter), BF16),
            pltpu.VMEM((sub * tp, ep * cap, quarter), BF16),
            pltpu.VMEM((ep * cap, width), BF16),
            pltpu.VMEM((ep * cap, hid), BF16),
            pltpu.VMEM((sub - 1, ep * cap, half), BF16),
            pltpu.VMEM((sub - 1, ep * cap, half), BF16),
            pltpu.VMEM((ep * cap, half), F32),
            pltpu.VMEM((tp, ep * cap, quarter), BF16),
            pltpu.VMEM((experts, cap, quarter), BF16),
            dma((3,)),
            dma((ep, tp)),
            dma((ep, tp)),
            dma((ep, sub - 1)),
            dma((ep, sub - 1)),
            dma((chunks, sub - 1)),
            dma((chunks, sub - 1)),
            dma((ep, tp)),
            dma((ep, tp)),
        ],
        compiler_params=pltpu.CompilerParams(
            collective_id=0, has_side_effects=True, vmem_limit_bytes=48 * 1024 * 1024
        ),
        cost_estimate=pl.CostEstimate(
            flops=2 * hops * ep * cap * hid * width * 3,
            bytes_accessed=3 * hid * width * 2,
            transcendentals=hops * ep * cap * hid,
        ),
    )(rows, path[:, :, 0], norm_gain, gate_weight, up_weight, down_weight)


def solution(mesh):
    ep, tp, sub = mesh.shape["ep"], mesh.shape["tp"], mesh.shape["sub"]

    def run(rows, path, norm_gain, gate_weight, up_weight, down_weight):
        cap = max(16, 2 * rows.shape[0] // (ep * tp))
        sizes = (ep, tp, sub, cap, ep // 2)
        return shards(sizes, rows, path, norm_gain, gate_weight, up_weight, down_weight)

    in_specs = (
        P(("groups", "ep"), ("sub", "tp")),
        P(None, ("groups", "ep"), None),
        P(("ep", "tp"), None),
        P(("ep", "tp"), "sub", None),
        P(("ep", "tp"), "sub", None),
        P(("ep", "tp"), "sub", None),
    )
    out_specs = P(("groups", "ep"), ("sub", "tp"))
    return jax.shard_map(run, mesh=mesh, in_specs=in_specs, out_specs=out_specs, check_vma=False)
```

time: 462 us -> 181 us (0.39)
  blocking collectives: 190 us -> 0 us
  waiting for transfers between devices: 181 us -> 0 us
  Pallas kernels: 0 us -> 177 us
  matrix products: 65.5 us -> 0 us
  between operations: 13.7 us -> 0.01 us
  other arithmetic: 10.2 us -> 0 us
    all_to_all x8 -> x0, blocking collectives: 190 us -> none  [the longest x4 118 us: shards(): lax.all_to_all(packed, 'ep', split_axis=0, concat_axis=0, tiled=True)]
    pallas_call x0 -> x1, Pallas kernels: none -> 177 us  [shards(): pl.pallas_call(functools.partial(chain_kernel, sizes), out_shape=jax.Shap...]
    reduce_scatter x8 -> x0, waiting for transfers between devices: 108 us -> none  [the longest x4 77.1 us: shards(): lax.psum_scatter(partial_value, 'sub', scatter_dimension=3, tiled=True)]
    all_gather x4 -> x0, waiting for transfers between devices: 72.1 us -> none  [shards(): whole = lax.all_gather(state, ('sub', 'tp'), axis=1, tiled=True)]
    dot_general x16 -> x0, matrix products: 65.5 us -> none  [the longest x4 36.1 us: expert_update(): jnp.einsum('slch,lhd->slcd', hidden, down_weight, preferred_element_type=...]
    convert_element_type x8 -> x0, other arithmetic: 7.2 us -> none  [the longest x4 6.88 us: shards(): (state.astype(jnp.float32) + update.astype(jnp.float32)).astype(jnp.bfloa...]
  transfers between devices with their start and end apart: 12 -> 0, of which waited for: 12 -> 0; matrix products, arithmetic and copies ran while one was open for 1% -> 0% of each run, Pallas kernels for 0% -> 0%
where the time goes in v1:
time: 181 us; the launch traced here: 180 us
  Pallas kernels  177 us (98%)
  local copies, waits for them, and re-layouts  3.05 us (2%)
    pallas_call x1, Pallas kernels, shards(): pl.pallas_call(functools.partial(chain_kernel, sizes), out_shape=jax.Shap...  177 us

profile of v1, /device:TPU:1, one launch (start us, length us, event | category | flops | bytes accessed | tf_op | source)
XLA Modules:
  0.0 180.3 jit_solution(3236301554367779482)
XLA Ops:
  0.0 0.0 copy-start
  0.0 0.9 copy-done
  1.0 0.0 copy-start.1
  1.0 0.7 copy-done.1
  1.7 0.0 copy-start.2
  1.7 0.7 copy-done.2
  2.4 177.2 %shard_map.64 = bf16[128,1024]{1,0:T(8,128)(2,1)S(1)} custom-call(bf16[128,1024]{1,0:T(8,128)(2,1)S(1)} %copy-done, s32[4,128]{1,0:T(4,128)S(1)} %bitcast.1, f32[1,4096]{1,0:T(1,128)S(1)} %copy-done.1, bf16[1,704,4096]{2,1,0:T(8,128)(2,1)} %gate_hbm.1, bf16[1,704,4096]{2,1,0:T(8,128)(2,1)} %up_hbm.1, bf16[1,704,4096]{2,1,0:T(8,128)(2,1)} %down_hbm.1), custom_call_target="tpu_custom_call" | custom-call | flops 8858370048 | bytes 17301504 | tf_op jit(solution)/shard_map/pallas_call | solution.py:303
  179.5 0.7 copy.8
Async XLA Ops:
  0.0 0.9 copy-start
  1.0 0.7 copy-start.1
  1.7 0.7 copy-start.2

commit v2 on v1

--- a/solution.py
+++ b/solution.py
@@ -24,17 +24,20 @@
 
 def chain_kernel(
     sizes,
-    rows_ref,
-    path_ref,
-    gain_ref,
+    rows_hbm,
+    path_hbm,
+    gain_hbm,
     gate_hbm,
     up_hbm,
     down_hbm,
     state_ref,
+    path_ref,
+    gain_ref,
     gate_ref,
     up_ref,
     down_ref,
     placing_ref,
+    taking_ref,
     packed_ref,
     arrived_ref,
     normed_ref,
@@ -54,20 +57,29 @@
     ret_send,
     ret_recv,
 ):
-    ep, tp, sub, cap, per_chunk = sizes
+    ep, tp, sub, cap = sizes
     z, s, t = lax.axis_index("ep"), lax.axis_index("sub"), lax.axis_index("tp")
     hops = path_ref.shape[0]
     local_rows, quarter = state_ref.shape
     half = quarter * tp
     experts = ep * tp
-    chunks = ep // per_chunk
-    chunk_rows = per_chunk * cap
+    chunks = ep // 2
+    pairs = [(chunks + i, i) for i in range(chunks)]
+    order = [k for pair in pairs for k in pair]
+    chunk_rows = 2 * cap
     here = s * tp + t
 
     loads = [
         pltpu.make_async_copy(src, dst, load_sem.at[i])
         for i, (src, dst) in enumerate(
-            ((gate_hbm, gate_ref), (up_hbm, up_ref), (down_hbm, down_ref))
+            (
+                (rows_hbm, state_ref),
+                (path_hbm, path_ref),
+                (gate_hbm, gate_ref),
+                (up_hbm, up_ref),
+                (down_hbm, down_ref),
+                (gain_hbm, gain_ref),
+            )
         )
     ]
     for load in loads:
@@ -91,7 +103,7 @@
         peers += 1
 
     def rows_of(k):
-        return pl.ds(k * cap, cap)
+        return pl.ds(order.index(k) * cap, cap)
 
     def rows_in(chunk):
         return pl.ds(chunk * chunk_rows, chunk_rows)
@@ -118,12 +130,12 @@
             device_id_type=MESH,
         )
 
-    def part_copy(chunk, j):
+    def part_copy(k, j):
         return pltpu.make_async_remote_copy(
-            src_ref=part_out_ref.at[j - 1, rows_in(chunk)],
-            dst_ref=part_in_ref.at[j - 1, rows_in(chunk)],
-            send_sem=part_send.at[chunk, j - 1],
-            recv_sem=part_recv.at[chunk, j - 1],
+            src_ref=part_out_ref.at[j - 1, rows_of(k)],
+            dst_ref=part_in_ref.at[j - 1, rows_of(k)],
+            send_sem=part_send.at[k, j - 1],
+            recv_sem=part_recv.at[k, j - 1],
             device_id={"sub": (s + j) % sub},
             device_id_type=MESH,
         )
@@ -140,6 +152,7 @@
         )
 
     remote = [(k, c) for k in range(ep) for c in range(tp) if k or c]
+    own_first = [0] + list(range(chunks, ep)) + list(range(1, chunks))
 
     def make_placing(hop):
         named = path_ref[pl.ds(hop, 1), :]
@@ -160,13 +173,19 @@
         placing_ref[hop] = jnp.where(slots.astype(F32) == target, 1.0, 0.0).astype(BF16)
 
     def dispatch(hop):
-        packed = jnp.dot(
-            placing_ref[hop], state_ref[...], preferred_element_type=F32
-        ).astype(BF16)
-        packed_ref[...] = packed.reshape(experts, cap, quarter)
-        for k, c in remote:
-            dispatch_copy(k, c).start()
-        arrived_ref[here, rows_of(0), :] = packed_ref[z * tp + t]
+        for k in own_first:
+            first = partner(z, k, ep) * tp
+            lines = pl.ds(pl.multiple_of(first * cap, 16), tp * cap)
+            packed = jnp.dot(
+                placing_ref[hop, lines, :], state_ref[...], preferred_element_type=F32
+            ).astype(BF16)
+            for i in range(tp):
+                packed_ref[first + i] = packed[i * cap : (i + 1) * cap]
+            for c in range(tp):
+                if k or c:
+                    dispatch_copy(k, c).start()
+                else:
+                    arrived_ref[here, rows_of(0), :] = packed_ref[z * tp + t]
 
     def forward(k):
         for c in range(tp):
@@ -191,7 +210,7 @@
             ).astype(BF16)
 
     def expand(chunk):
-        for k in range(chunk * per_chunk, (chunk + 1) * per_chunk):
+        for k in pairs[chunk]:
             normalise(k)
         normed = normed_ref[rows_in(chunk), :]
         dims = (((1,), (1,)), ((), ()))
@@ -221,13 +240,14 @@
     def project(chunk):
         for j in range(1, sub):
             contract(chunk, j, part_out_ref.at[j - 1])
-            part_copy(chunk, j).start()
+            for k in pairs[chunk]:
+                part_copy(k, j).start()
         contract(chunk, 0, own_ref)
 
     def give_back(chunk):
-        for j in range(1, sub):
-            part_copy(chunk, j).wait_recv()
-        for k in range(chunk * per_chunk, (chunk + 1) * per_chunk):
+        for k in pairs[chunk]:
+            for j in range(1, sub):
+                part_copy(k, j).wait_recv()
             for i in range(tp):
                 columns = pl.ds(i * quarter, quarter)
                 value = own_ref[rows_of(k), columns]
@@ -240,41 +260,40 @@
                 else:
                     returned_ref[z * tp + t] = summed_ref[t, rows_of(k), :]
 
-    state_ref[...] = rows_ref[...]
+    for load in loads[:2]:
+        load.wait()
     make_placing(0)
     pl.semaphore_wait(barrier, peers)
     dispatch(0)
     for hop in range(1, hops):
         make_placing(hop)
-    for load in loads:
+    for hop in range(hops):
+        taking_ref[hop] = placing_ref[hop].T
+    for load in loads[2:]:
         load.wait()
 
     def one_hop(hop, carry):
-        for k in range(per_chunk):
+        for k in pairs[0][::-1]:
             forward(k)
         expand(0)
-        for k in range(per_chunk, ep):
-            forward(k)
-        project(0)
         for chunk in range(1, chunks):
+            for k in pairs[chunk][::-1]:
+                forward(k)
+            project(chunk - 1)
             expand(chunk)
-            project(chunk)
-        for k, c in remote:
-            dispatch_copy(k, c).wait_send()
+        project(chunks - 1)
         for k in range(ep):
             for j in range(1, sub):
                 forward_copy(k, j).wait_send()
         for chunk in range(chunks):
             give_back(chunk)
-        for chunk in range(chunks):
-            for j in range(1, sub):
-                part_copy(chunk, j).wait_send()
+        for k, c in remote:
+            dispatch_copy(k, c).wait_send()
         for k, c in remote:
             return_copy(k, c).wait_recv()
-        update = lax.dot_general(
-            placing_ref[hop],
+        update = jnp.dot(
+            taking_ref[hop],
             returned_ref[...].reshape(experts * cap, quarter),
-            (((0,), (0,)), ((), ())),
             preferred_element_type=F32,
         )
         state_ref[...] = (state_ref[...].astype(F32) + update).astype(BF16)
@@ -283,6 +302,9 @@
         def _():
             dispatch(hop + 1)
 
+        for k in range(ep):
+            for j in range(1, sub):
+                part_copy(k, j).wait_send()
         for k, c in remote:
             return_copy(k, c).wait_send()
         return carry
@@ -291,25 +313,27 @@
 
 
 def shards(sizes, rows, path, norm_gain, gate_weight, up_weight, down_weight):
-    ep, tp, sub, cap, per_chunk = sizes
+    ep, tp, sub, cap = sizes
     local_rows, quarter = rows.shape
     hops = path.shape[0]
     hid, width = gate_weight.shape[1:]
     half = quarter * tp
     experts = ep * tp
-    chunks = ep // per_chunk
     dma = pltpu.SemaphoreType.DMA
     vmem, any_space = pl.BlockSpec(memory_space=pltpu.VMEM), pl.BlockSpec(memory_space=pl.ANY)
     return pl.pallas_call(
         functools.partial(chain_kernel, sizes),
         out_shape=jax.ShapeDtypeStruct(rows.shape, rows.dtype),
-        in_specs=[vmem, vmem, vmem, any_space, any_space, any_space],
+        in_specs=[any_space] * 6,
         out_specs=vmem,
         scratch_shapes=[
+            pltpu.VMEM((hops, local_rows), jnp.int32),
+            pltpu.VMEM((1, width), F32),
             pltpu.VMEM((1, hid, width), BF16),
             pltpu.VMEM((1, hid, width), BF16),
             pltpu.VMEM((1, hid, width), BF16),
             pltpu.VMEM((hops, experts * cap, local_rows), BF16),
+            pltpu.VMEM((hops, local_rows, experts * cap), BF16),
             pltpu.VMEM((experts, cap, quarter), BF16),
             pltpu.VMEM((sub * tp, ep * cap, quarter), BF16),
             pltpu.VMEM((ep * cap, width), BF16),
@@ -319,18 +343,18 @@
             pltpu.VMEM((ep * cap, half), F32),
             pltpu.VMEM((tp, ep * cap, quarter), BF16),
             pltpu.VMEM((experts, cap, quarter), BF16),
-            dma((3,)),
+            dma((6,)),
             dma((ep, tp)),
             dma((ep, tp)),
             dma((ep, sub - 1)),
             dma((ep, sub - 1)),
-            dma((chunks, sub - 1)),
-            dma((chunks, sub - 1)),
+            dma((ep, sub - 1)),
+            dma((ep, sub - 1)),
             dma((ep, tp)),
             dma((ep, tp)),
         ],
         compiler_params=pltpu.CompilerParams(
-            collective_id=0, has_side_effects=True, vmem_limit_bytes=48 * 1024 * 1024
+            collective_id=0, has_side_effects=True, vmem_limit_bytes=56 * 1024 * 1024
         ),
         cost_estimate=pl.CostEstimate(
             flops=2 * hops * ep * cap * hid * width * 3,
@@ -345,7 +369,7 @@
 
     def run(rows, path, norm_gain, gate_weight, up_weight, down_weight):
         cap = max(16, 2 * rows.shape[0] // (ep * tp))
-        sizes = (ep, tp, sub, cap, ep // 2)
+        sizes = (ep, tp, sub, cap)
         return shards(sizes, rows, path, norm_gain, gate_weight, up_weight, down_weight)
 
     in_specs = (

time: 181 us -> 178 us (0.983)
  no operation moved by 1% of the time
where the time goes in v2:
time: 178 us; the launch traced here: 177 us
  Pallas kernels  176 us (99%)
    pallas_call x1, Pallas kernels, shards(): pl.pallas_call(functools.partial(chain_kernel, sizes), out_shape=jax.Shap...  176 us

profile of v2, /device:TPU:1, one launch (start us, length us, event | category | flops | bytes accessed | tf_op | source)
XLA Modules:
  0.0 177.4 jit_solution(5268159889699562813)
XLA Ops:
  0.0 175.7 %shard_map.64 = bf16[128,1024]{1,0:T(8,128)(2,1)} custom-call(bf16[128,1024]{1,0:T(8,128)(2,1)} %rows_hbm.1, s32[4,128]{1,0:T(4,128)} %bitcast.1, f32[1,4096]{1,0:T(1,128)} %gain_hbm.1, bf16[1,704,4096]{2,1,0:T(8,128)(2,1)} %gate_hbm.1, bf16[1,704,4096]{2,1,0:T(8,128)(2,1)} %up_hbm.1, bf16[1,704,4096]{2,1,0:T(8,128)(2,1)} %down_hbm.1), custom_call_target="tpu_custom_call" | custom-call | flops 8858370048 | bytes 17301504 | tf_op jit(solution)/shard_map/pallas_call | solution.py:324
  175.7 1.7 copy.8

commit v3 on v2

--- a/solution.py
+++ b/solution.py
@@ -36,6 +36,7 @@
     gate_ref,
     up_ref,
     down_ref,
+    turned_ref,
     placing_ref,
     taking_ref,
     packed_ref,
@@ -214,11 +215,9 @@
             normalise(k)
         normed = normed_ref[rows_in(chunk), :]
         dims = (((1,), (1,)), ((), ()))
-        gate = lax.dot_general(normed, gate_ref[0], dims, preferred_element_type=F32)
-        upward = lax.dot_general(normed, up_ref[0], dims, preferred_element_type=F32)
-        hidden_ref[rows_in(chunk), :] = (
-            gate / (1.0 + jnp.exp(-gate)) * upward
-        ).astype(BF16)
+        gate = lax.dot_general(gate_ref[0], normed, dims, preferred_element_type=F32)
+        upward = lax.dot_general(up_ref[0], normed, dims, preferred_element_type=F32)
+        hidden_ref[chunk] = (gate / (1.0 + jnp.exp(-gate)) * upward).astype(BF16)
 
     tile = min(512, half)
 
@@ -228,11 +227,10 @@
         def step(i, carry):
             inside = pl.ds(pl.multiple_of(i * tile, tile), tile)
             columns = pl.ds(pl.multiple_of(base + i * tile, tile), tile)
-            out[rows_in(chunk), inside] = jnp.dot(
-                hidden_ref[rows_in(chunk), :],
-                down_ref[0, :, columns],
-                preferred_element_type=F32,
-            ).astype(out.dtype)
+            product = jnp.dot(
+                turned_ref[columns, :], hidden_ref[chunk], preferred_element_type=F32
+            )
+            out[rows_in(chunk), inside] = product.T.astype(out.dtype)
             return carry
 
         lax.fori_loop(0, half // tile, step, 0)
@@ -271,6 +269,13 @@
         taking_ref[hop] = placing_ref[hop].T
     for load in loads[2:]:
         load.wait()
+
+    def turn(i, carry):
+        columns = pl.ds(pl.multiple_of(i * tile, tile), tile)
+        turned_ref[columns, :] = down_ref[0, :, columns].T
+        return carry
+
+    lax.fori_loop(0, turned_ref.shape[0] // tile, turn, 0)
 
     def one_hop(hop, carry):
         for k in pairs[0][::-1]:
@@ -332,12 +337,13 @@
             pltpu.VMEM((1, hid, width), BF16),
             pltpu.VMEM((1, hid, width), BF16),
             pltpu.VMEM((1, hid, width), BF16),
+            pltpu.VMEM((width, hid), BF16),
             pltpu.VMEM((hops, experts * cap, local_rows), BF16),
             pltpu.VMEM((hops, local_rows, experts * cap), BF16),
             pltpu.VMEM((experts, cap, quarter), BF16),
             pltpu.VMEM((sub * tp, ep * cap, quarter), BF16),
             pltpu.VMEM((ep * cap, width), BF16),
-            pltpu.VMEM((ep * cap, hid), BF16),
+            pltpu.VMEM((ep // 2, hid, 2 * cap), BF16),
             pltpu.VMEM((sub - 1, ep * cap, half), BF16),
             pltpu.VMEM((sub - 1, ep * cap, half), BF16),
             pltpu.VMEM((ep * cap, half), F32),

time: 178 us -> 179 us (level)
  no operation moved by 1% of the time
where the time goes in v3:
time: 179 us
  Pallas kernels  177 us (99%)
    pallas_call x1, Pallas kernels, shards(): pl.pallas_call(functools.partial(chain_kernel, sizes), out_shape=jax.Shap...  177 us

profile of v3, /device:TPU:1, one launch (start us, length us, event | category | flops | bytes accessed | tf_op | source)
XLA Modules:
  0.0 178.5 jit_solution(12398692445430832067)
XLA Ops:
  0.0 176.8 %shard_map.64 = bf16[128,1024]{1,0:T(8,128)(2,1)} custom-call(bf16[128,1024]{1,0:T(8,128)(2,1)} %rows_hbm.1, s32[4,128]{1,0:T(4,128)} %bitcast.1, f32[1,4096]{1,0:T(1,128)} %gain_hbm.1, bf16[1,704,4096]{2,1,0:T(8,128)(2,1)} %gate_hbm.1, bf16[1,704,4096]{2,1,0:T(8,128)(2,1)} %up_hbm.1, bf16[1,704,4096]{2,1,0:T(8,128)(2,1)} %down_hbm.1), custom_call_target="tpu_custom_call" | custom-call | flops 8858370048 | bytes 17301504 | tf_op jit(solution)/shard_map/pallas_call | solution.py:329
  176.8 1.7 copy.8

commit v4 on v3

--- a/solution.py
+++ b/solution.py
@@ -182,18 +182,33 @@
             ).astype(BF16)
             for i in range(tp):
                 packed_ref[first + i] = packed[i * cap : (i + 1) * cap]
-            for c in range(tp):
-                if k or c:
-                    dispatch_copy(k, c).start()
-                else:
-                    arrived_ref[here, rows_of(0), :] = packed_ref[z * tp + t]
-
-    def forward(k):
+        arrived_ref[here, rows_of(0), :] = packed_ref[z * tp + t]
+        send(0)
+
+    def send(k):
+        for c in range(tp):
+            if k or c:
+                dispatch_copy(k, c).start()
+
+    def arrive(k):
         for c in range(tp):
             if k or c:
                 dispatch_copy(k, c).wait_recv()
+
+    def forward(k):
         for j in range(1, sub):
             forward_copy(k, j).start()
+
+    def either(first, second):
+        @pl.when(t % 2 == 0)
+        def _():
+            first()
+            second()
+
+        @pl.when(t % 2 == 1)
+        def _():
+            second()
+            first()
 
     def normalise(k):
         for j in range(1, sub):
@@ -238,11 +253,14 @@
     def project(chunk):
         for j in range(1, sub):
             contract(chunk, j, part_out_ref.at[j - 1])
-            for k in pairs[chunk]:
+        contract(chunk, 0, own_ref)
+
+    def exchange(chunk):
+        for k in pairs[chunk]:
+            for j in range(1, sub):
                 part_copy(k, j).start()
-        contract(chunk, 0, own_ref)
-
-    def give_back(chunk):
+
+    def sum_up(chunk):
         for k in pairs[chunk]:
             for j in range(1, sub):
                 part_copy(k, j).wait_recv()
@@ -252,11 +270,14 @@
                 for j in range(1, sub):
                     value = value + part_in_ref[j - 1, rows_of(k), columns].astype(F32)
                 summed_ref[i, rows_of(k), :] = value.astype(BF16)
+            if not k:
+                returned_ref[z * tp + t] = summed_ref[t, rows_of(k), :]
+
+    def give_back(chunk):
+        for k in pairs[chunk]:
             for c in range(tp):
                 if k or c:
                     return_copy(k, c).start()
-                else:
-                    returned_ref[z * tp + t] = summed_ref[t, rows_of(k), :]
 
     for load in loads[:2]:
         load.wait()
@@ -277,21 +298,42 @@
 
     lax.fori_loop(0, turned_ref.shape[0] // tile, turn, 0)
 
+    last = chunks - 1
+
+    def own_block():
+        arrive(0)
+        forward(0)
+
     def one_hop(hop, carry):
-        for k in pairs[0][::-1]:
-            forward(k)
-        expand(0)
-        for chunk in range(1, chunks):
-            for k in pairs[chunk][::-1]:
+        either(lambda: send(pairs[0][0]), own_block)
+        for i in range(1, chunks):
+            far, near = pairs[i - 1]
+            arrive(far)
+            either(lambda: send(pairs[i][0]), lambda: forward(far))
+            send(pairs[i][1])
+            if i >= 2:
+                arrive(near)
+                forward(near)
+                project(i - 2)
+                exchange(i - 2)
+            expand(i - 1)
+        for k in pairs[last]:
+            if k:
+                arrive(k)
                 forward(k)
-            project(chunk - 1)
-            expand(chunk)
-        project(chunks - 1)
+        if last:
+            project(last - 1)
+            exchange(last - 1)
+        expand(last)
         for k in range(ep):
             for j in range(1, sub):
                 forward_copy(k, j).wait_send()
-        for chunk in range(chunks):
-            give_back(chunk)
+        for chunk in range(last):
+            sum_up(chunk)
+        project(last)
+        either(lambda: exchange(last), lambda: [give_back(chunk) for chunk in range(last)])
+        sum_up(last)
+        give_back(last)
         for k, c in remote:
             dispatch_copy(k, c).wait_send()
         for k, c in remote:

time: 179 us -> 196 us (1.095)
  Pallas kernels: 177 us -> 194 us
    pallas_call x1, Pallas kernels: 177 us -> 194 us  [shards(): pl.pallas_call(functools.partial(chain_kernel, sizes), out_shape=jax.Shap...]
where the time goes in v4:
time: 196 us; the launch traced here: 195 us
  Pallas kernels  194 us (99%)
    pallas_call x1, Pallas kernels, shards(): pl.pallas_call(functools.partial(chain_kernel, sizes), out_shape=jax.Shap...  194 us

profile of v4, /device:TPU:1, one launch (start us, length us, event | category | flops | bytes accessed | tf_op | source)
XLA Modules:
  0.0 195.4 jit_solution(15114778007799340919)
XLA Ops:
  0.0 193.7 %shard_map.64 = bf16[128,1024]{1,0:T(8,128)(2,1)} custom-call(bf16[128,1024]{1,0:T(8,128)(2,1)} %rows_hbm.1, s32[4,128]{1,0:T(4,128)} %bitcast.1, f32[1,4096]{1,0:T(1,128)} %gain_hbm.1, bf16[1,704,4096]{2,1,0:T(8,128)(2,1)} %gate_hbm.1, bf16[1,704,4096]{2,1,0:T(8,128)(2,1)} %up_hbm.1, bf16[1,704,4096]{2,1,0:T(8,128)(2,1)} %down_hbm.1), custom_call_target="tpu_custom_call" | custom-call | flops 8858370048 | bytes 17301504 | tf_op jit(solution)/shard_map/pallas_call | solution.py:371
  193.7 1.7 copy.8

commit v5 on v3

--- a/solution.py
+++ b/solution.py
@@ -64,10 +64,8 @@
     local_rows, quarter = state_ref.shape
     half = quarter * tp
     experts = ep * tp
-    chunks = ep // 2
-    pairs = [(chunks + i, i) for i in range(chunks)]
-    order = [k for pair in pairs for k in pair]
-    chunk_rows = 2 * cap
+    far, near = list(range(ep // 2, ep)), list(range(1, ep // 2))
+    order = far + near + [0]
     here = s * tp + t
 
     loads = [
@@ -106,9 +104,6 @@
     def rows_of(k):
         return pl.ds(order.index(k) * cap, cap)
 
-    def rows_in(chunk):
-        return pl.ds(chunk * chunk_rows, chunk_rows)
-
     def dispatch_copy(k, c):
         to_z, to_t = partner(z, k, ep), (t + c) % tp
         return pltpu.make_async_remote_copy(
@@ -120,23 +115,23 @@
             device_id_type=MESH,
         )
 
-    def forward_copy(k, j):
-        block = arrived_ref.at[pl.ds(s * tp, tp), rows_of(k)]
+    def forward_copy(k, c, j):
+        block = arrived_ref.at[s * tp + (t + tp - c) % tp, rows_of(k)]
         return pltpu.make_async_remote_copy(
             src_ref=block,
             dst_ref=block,
-            send_sem=fwd_send.at[k, j - 1],
-            recv_sem=fwd_recv.at[k, j - 1],
+            send_sem=fwd_send.at[k, c, j - 1],
+            recv_sem=fwd_recv.at[k, c, j - 1],
             device_id={"sub": (s + j) % sub},
             device_id_type=MESH,
         )
 
-    def part_copy(k, j):
+    def part_copy(k, c, j):
         return pltpu.make_async_remote_copy(
-            src_ref=part_out_ref.at[j - 1, rows_of(k)],
-            dst_ref=part_in_ref.at[j - 1, rows_of(k)],
-            send_sem=part_send.at[k, j - 1],
-            recv_sem=part_recv.at[k, j - 1],
+            src_ref=part_out_ref.at[j - 1, c, rows_of(k)],
+            dst_ref=part_in_ref.at[j - 1, c, rows_of(k)],
+            send_sem=part_send.at[k, c, j - 1],
+            recv_sem=part_recv.at[k, c, j - 1],
             device_id={"sub": (s + j) % sub},
             device_id_type=MESH,
         )
@@ -144,7 +139,7 @@
     def return_copy(k, c):
         to_z, to_t = partner(z, k, ep), (t + c) % tp
         return pltpu.make_async_remote_copy(
-            src_ref=summed_ref.at[to_t, rows_of(k)],
+            src_ref=summed_ref.at[c, rows_of(k)],
             dst_ref=returned_ref.at[z * tp + t],
             send_sem=ret_send.at[k, c],
             recv_sem=ret_recv.at[k, c],
@@ -152,8 +147,8 @@
             device_id_type=MESH,
         )
 
-    remote = [(k, c) for k in range(ep) for c in range(tp) if k or c]
-    own_first = [0] + list(range(chunks, ep)) + list(range(1, chunks))
+    cores, others = range(tp), range(1, sub)
+    remote = [(k, c) for k in order for c in cores if k or c]
 
     def make_placing(hop):
         named = path_ref[pl.ds(hop, 1), :]
@@ -174,7 +169,7 @@
         placing_ref[hop] = jnp.where(slots.astype(F32) == target, 1.0, 0.0).astype(BF16)
 
     def dispatch(hop):
-        for k in own_first:
+        for k in [0] + order[:-1]:
             first = partner(z, k, ep) * tp
             lines = pl.ds(pl.multiple_of(first * cap, 16), tp * cap)
             packed = jnp.dot(
@@ -189,15 +184,16 @@
                     arrived_ref[here, rows_of(0), :] = packed_ref[z * tp + t]
 
     def forward(k):
-        for c in range(tp):
+        for c in cores:
             if k or c:
                 dispatch_copy(k, c).wait_recv()
-        for j in range(1, sub):
-            forward_copy(k, j).start()
+            for j in others:
+                forward_copy(k, c, j).start()
 
     def normalise(k):
-        for j in range(1, sub):
-            forward_copy(k, j).wait_recv()
+        for c in cores:
+            for j in others:
+                forward_copy(k, c, j).wait_recv()
         total = jnp.zeros((cap, 1), F32)
         for q in range(sub * tp):
             value = arrived_ref[q, rows_of(k), :].astype(F32)
@@ -210,53 +206,40 @@
                 value * scale * gain_ref[:, columns]
             ).astype(BF16)
 
-    def expand(chunk):
-        for k in pairs[chunk]:
-            normalise(k)
-        normed = normed_ref[rows_in(chunk), :]
+    def expand():
+        normed = normed_ref[...]
         dims = (((1,), (1,)), ((), ()))
         gate = lax.dot_general(gate_ref[0], normed, dims, preferred_element_type=F32)
         upward = lax.dot_general(up_ref[0], normed, dims, preferred_element_type=F32)
-        hidden_ref[chunk] = (gate / (1.0 + jnp.exp(-gate)) * upward).astype(BF16)
-
-    tile = min(512, half)
-
-    def contract(chunk, j, out):
-        base = ((s + j) % sub) * half
+        hidden_ref[...] = (gate / (1.0 + jnp.exp(-gate)) * upward).astype(BF16)
+
+    tile = min(512, quarter)
+
+    def contract(j, c, out):
+        base = ((s + j) % sub) * half + (t + c) % tp * quarter
 
         def step(i, carry):
             inside = pl.ds(pl.multiple_of(i * tile, tile), tile)
             columns = pl.ds(pl.multiple_of(base + i * tile, tile), tile)
             product = jnp.dot(
-                turned_ref[columns, :], hidden_ref[chunk], preferred_element_type=F32
+                turned_ref[columns, :], hidden_ref[...], preferred_element_type=F32
             )
-            out[rows_in(chunk), inside] = product.T.astype(out.dtype)
+            out[:, inside] = product.T.astype(out.dtype)
             return carry
 
-        lax.fori_loop(0, half // tile, step, 0)
-
-    def project(chunk):
-        for j in range(1, sub):
-            contract(chunk, j, part_out_ref.at[j - 1])
-            for k in pairs[chunk]:
-                part_copy(k, j).start()
-        contract(chunk, 0, own_ref)
-
-    def give_back(chunk):
-        for k in pairs[chunk]:
-            for j in range(1, sub):
-                part_copy(k, j).wait_recv()
-            for i in range(tp):
-                columns = pl.ds(i * quarter, quarter)
-                value = own_ref[rows_of(k), columns]
-                for j in range(1, sub):
-                    value = value + part_in_ref[j - 1, rows_of(k), columns].astype(F32)
-                summed_ref[i, rows_of(k), :] = value.astype(BF16)
-            for c in range(tp):
-                if k or c:
-                    return_copy(k, c).start()
-                else:
-                    returned_ref[z * tp + t] = summed_ref[t, rows_of(k), :]
+        lax.fori_loop(0, quarter // tile, step, 0)
+
+    def give_back(k, c):
+        for j in others:
+            part_copy(k, c, j).wait_recv()
+        value = own_ref[c, rows_of(k), :]
+        for j in others:
+            value = value + part_in_ref[j - 1, c, rows_of(k), :].astype(F32)
+        summed_ref[c, rows_of(k), :] = value.astype(BF16)
+        if k or c:
+            return_copy(k, c).start()
+        else:
+            returned_ref[z * tp + t] = summed_ref[0, rows_of(k), :]
 
     for load in loads[:2]:
         load.wait()
@@ -278,20 +261,28 @@
     lax.fori_loop(0, turned_ref.shape[0] // tile, turn, 0)
 
     def one_hop(hop, carry):
-        for k in pairs[0][::-1]:
+        forward(0)
+        forward(far[0])
+        for k, ahead in zip(near, far[1:]):
             forward(k)
-        expand(0)
-        for chunk in range(1, chunks):
-            for k in pairs[chunk][::-1]:
-                forward(k)
-            project(chunk - 1)
-            expand(chunk)
-        project(chunks - 1)
-        for k in range(ep):
-            for j in range(1, sub):
-                forward_copy(k, j).wait_send()
-        for chunk in range(chunks):
-            give_back(chunk)
+            forward(ahead)
+        for k in [0] + near + far:
+            normalise(k)
+        expand()
+        for c in cores:
+            for j in others:
+                contract(j, c, part_out_ref.at[j - 1, c])
+                for k in order:
+                    part_copy(k, c, j).start()
+        for c in cores:
+            contract(0, c, own_ref.at[c])
+        for k in order:
+            for c in cores:
+                for j in others:
+                    forward_copy(k, c, j).wait_send()
+        for c in cores:
+            for k in order:
+                give_back(k, c)
         for k, c in remote:
             dispatch_copy(k, c).wait_send()
         for k, c in remote:
@@ -307,9 +298,10 @@
         def _():
             dispatch(hop + 1)
 
-        for k in range(ep):
-            for j in range(1, sub):
-                part_copy(k, j).wait_send()
+        for k in order:
+            for c in cores:
+                for j in others:
+                    part_copy(k, c, j).wait_send()
         for k, c in remote:
             return_copy(k, c).wait_send()
         return carry
@@ -322,7 +314,6 @@
     local_rows, quarter = rows.shape
     hops = path.shape[0]
     hid, width = gate_weight.shape[1:]
-    half = quarter * tp
     experts = ep * tp
     dma = pltpu.SemaphoreType.DMA
     vmem, any_space = pl.BlockSpec(memory_space=pltpu.VMEM), pl.BlockSpec(memory_space=pl.ANY)
@@ -343,19 +334,19 @@
             pltpu.VMEM((experts, cap, quarter), BF16),
             pltpu.VMEM((sub * tp, ep * cap, quarter), BF16),
             pltpu.VMEM((ep * cap, width), BF16),
-            pltpu.VMEM((ep // 2, hid, 2 * cap), BF16),
-            pltpu.VMEM((sub - 1, ep * cap, half), BF16),
-            pltpu.VMEM((sub - 1, ep * cap, half), BF16),
-            pltpu.VMEM((ep * cap, half), F32),
+            pltpu.VMEM((hid, ep * cap), BF16),
+            pltpu.VMEM((sub - 1, tp, ep * cap, quarter), BF16),
+            pltpu.VMEM((sub - 1, tp, ep * cap, quarter), BF16),
+            pltpu.VMEM((tp, ep * cap, quarter), F32),
             pltpu.VMEM((tp, ep * cap, quarter), BF16),
             pltpu.VMEM((experts, cap, quarter), BF16),
             dma((6,)),
             dma((ep, tp)),
             dma((ep, tp)),
-            dma((ep, sub - 1)),
-            dma((ep, sub - 1)),
-            dma((ep, sub - 1)),
-            dma((ep, sub - 1)),
+            dma((ep, tp, sub - 1)),
+            dma((ep, tp, sub - 1)),
+            dma((ep, tp, sub - 1)),
+            dma((ep, tp, sub - 1)),
             dma((ep, tp)),
             dma((ep, tp)),
         ],

time: 179 us -> 160 us (0.89)
  Pallas kernels: 177 us -> 158 us
    pallas_call x1, Pallas kernels: 177 us -> 158 us  [shards(): pl.pallas_call(functools.partial(chain_kernel, sizes), out_shape=jax.Shap...]
where the time goes in v5:
time: 160 us
  Pallas kernels  158 us (99%)
  local copies, waits for them, and re-layouts  1.67 us (1%)
    pallas_call x1, Pallas kernels, shards(): pl.pallas_call(functools.partial(chain_kernel, sizes), out_shape=jax.Shap...  158 us

profile of v5, /device:TPU:1, one launch (start us, length us, event | category | flops | bytes accessed | tf_op | source)
XLA Modules:
  0.0 159.8 jit_solution(9475904735740549166)
XLA Ops:
  0.0 158.1 %shard_map.64 = bf16[128,1024]{1,0:T(8,128)(2,1)} custom-call(bf16[128,1024]{1,0:T(8,128)(2,1)} %rows_hbm.1, s32[4,128]{1,0:T(4,128)} %bitcast.1, f32[1,4096]{1,0:T(1,128)} %gain_hbm.1, bf16[1,704,4096]{2,1,0:T(8,128)(2,1)} %gate_hbm.1, bf16[1,704,4096]{2,1,0:T(8,128)(2,1)} %up_hbm.1, bf16[1,704,4096]{2,1,0:T(8,128)(2,1)} %down_hbm.1), custom_call_target="tpu_custom_call" | custom-call | flops 8858370048 | bytes 17301504 | tf_op jit(solution)/shard_map/pallas_call | solution.py:320
  158.1 1.7 %copy.8 = bf16[128,1024]{1,0:T(8,128)(2,1)} copy(bf16[128,1024]{1,0:T(8,128)(2,1)} %shard_map.64) | data formatting | bytes 524288

commit v6 on v5

--- a/solution.py
+++ b/solution.py
@@ -8,6 +8,7 @@
 from jax.sharding import PartitionSpec as P
 
 EPS = 1e-06
+LANES = 128
 MESH = pl.DeviceIdType.MESH
 F32 = jnp.float32
 BF16 = jnp.bfloat16
@@ -42,6 +43,9 @@
     packed_ref,
     arrived_ref,
     normed_ref,
+    squares_ref,
+    gate_acc,
+    up_acc,
     hidden_ref,
     part_out_ref,
     part_in_ref,
@@ -190,27 +194,42 @@
             for j in others:
                 forward_copy(k, c, j).start()
 
-    def normalise(k):
-        for c in cores:
-            for j in others:
-                forward_copy(k, c, j).wait_recv()
-        total = jnp.zeros((cap, 1), F32)
-        for q in range(sub * tp):
+    def weigh(k, j):
+        section = (s + sub - j) % sub
+        squares = jnp.zeros((cap, LANES), F32)
+        for i in cores:
+            q = section * tp + i
             value = arrived_ref[q, rows_of(k), :].astype(F32)
-            total = total + jnp.sum(value * value, axis=-1, keepdims=True)
-        scale = lax.rsqrt(total / float(quarter * sub * tp) + EPS)
-        for q in range(sub * tp):
-            value = arrived_ref[q, rows_of(k), :].astype(F32)
-            columns = pl.ds(q * quarter, quarter)
-            normed_ref[rows_of(k), columns] = (
-                value * scale * gain_ref[:, columns]
+            for lane in range(0, quarter, LANES):
+                piece = value[:, lane : lane + LANES]
+                squares = squares + piece * piece
+            columns = pl.ds(pl.multiple_of(q * quarter, LANES), quarter)
+            normed_ref[j, rows_of(k), pl.ds(i * quarter, quarter)] = (
+                value * gain_ref[:, columns]
             ).astype(BF16)
+        if j:
+            squares = squares + squares_ref[rows_of(k), :]
+        squares_ref[rows_of(k), :] = squares
 
     def expand():
-        normed = normed_ref[...]
         dims = (((1,), (1,)), ((), ()))
-        gate = lax.dot_general(gate_ref[0], normed, dims, preferred_element_type=F32)
-        upward = lax.dot_general(up_ref[0], normed, dims, preferred_element_type=F32)
+        for j in range(sub):
+            if j:
+                for k in order:
+                    for c in cores:
+                        forward_copy(k, c, j).wait_recv()
+            for k in order:
+                weigh(k, j)
+            section = (s + sub - j) % sub
+            columns = pl.ds(pl.multiple_of(section * half, LANES), half)
+            for acc, weight_ref in ((gate_acc, gate_ref), (up_acc, up_ref)):
+                product = lax.dot_general(
+                    weight_ref[0, :, columns], normed_ref[j], dims, preferred_element_type=F32
+                )
+                acc[...] = acc[...] + product if j else product
+        total = jnp.sum(squares_ref[...].T, axis=0, keepdims=True)
+        scale = lax.rsqrt(total / float(half * sub) + EPS)
+        gate, upward = gate_acc[...] * scale, up_acc[...] * scale
         hidden_ref[...] = (gate / (1.0 + jnp.exp(-gate)) * upward).astype(BF16)
 
     tile = min(512, quarter)
@@ -266,8 +285,6 @@
         for k, ahead in zip(near, far[1:]):
             forward(k)
             forward(ahead)
-        for k in [0] + near + far:
-            normalise(k)
         expand()
         for c in cores:
             for j in others:
@@ -333,7 +350,10 @@
             pltpu.VMEM((hops, local_rows, experts * cap), BF16),
             pltpu.VMEM((experts, cap, quarter), BF16),
             pltpu.VMEM((sub * tp, ep * cap, quarter), BF16),
-            pltpu.VMEM((ep * cap, width), BF16),
+            pltpu.VMEM((sub, ep * cap, width // sub), BF16),
+            pltpu.VMEM((ep * cap, LANES), F32),
+            pltpu.VMEM((hid, ep * cap), F32),
+            pltpu.VMEM((hid, ep * cap), F32),
             pltpu.VMEM((hid, ep * cap), BF16),
             pltpu.VMEM((sub - 1, tp, ep * cap, quarter), BF16),
             pltpu.VMEM((sub - 1, tp, ep * cap, quarter), BF16),

time: 160 us -> 154 us (0.963)
  Pallas kernels: 158 us -> 152 us
    pallas_call x1, Pallas kernels: 158 us -> 152 us  [shards(): pl.pallas_call(functools.partial(chain_kernel, sizes), out_shape=jax.Shap...]
where the time goes in v6:
time: 154 us; the launch traced here: 153 us
  Pallas kernels  152 us (99%)
  local copies, waits for them, and re-layouts  1.67 us (1%)
    pallas_call x1, Pallas kernels, shards(): pl.pallas_call(functools.partial(chain_kernel, sizes), out_shape=jax.Shap...  152 us

profile of v6, /device:TPU:1, one launch (start us, length us, event | category | flops | bytes accessed | tf_op | source)
XLA Modules:
  0.0 153.5 jit_solution(15675554004957904065)
XLA Ops:
  0.0 151.8 %shard_map.64 = bf16[128,1024]{1,0:T(8,128)(2,1)} custom-call(bf16[128,1024]{1,0:T(8,128)(2,1)} %rows_hbm.1, s32[4,128]{1,0:T(4,128)} %bitcast.1, f32[1,4096]{1,0:T(1,128)} %gain_hbm.1, bf16[1,704,4096]{2,1,0:T(8,128)(2,1)} %gate_hbm.1, bf16[1,704,4096]{2,1,0:T(8,128)(2,1)} %up_hbm.1, bf16[1,704,4096]{2,1,0:T(8,128)(2,1)} %down_hbm.1), custom_call_target="tpu_custom_call" | custom-call | flops 8858370048 | bytes 17301504 | tf_op jit(solution)/shard_map/pallas_call | solution.py:337
  151.8 1.7 %copy.8 = bf16[128,1024]{1,0:T(8,128)(2,1)} copy(bf16[128,1024]{1,0:T(8,128)(2,1)} %shard_map.64) | data formatting | bytes 524288

commit v7 on v6

--- a/solution.py
+++ b/solution.py
@@ -70,6 +70,7 @@
     experts = ep * tp
     far, near = list(range(ep // 2, ep)), list(range(1, ep // 2))
     order = far + near + [0]
+    coming = [k for pair in zip([0] + near, far) for k in pair]
     here = s * tp + t
 
     loads = [
@@ -173,19 +174,20 @@
         placing_ref[hop] = jnp.where(slots.astype(F32) == target, 1.0, 0.0).astype(BF16)
 
     def dispatch(hop):
-        for k in [0] + order[:-1]:
-            first = partner(z, k, ep) * tp
-            lines = pl.ds(pl.multiple_of(first * cap, 16), tp * cap)
+        line = ep // 2
+        for blocks, side in ((far, 1 - z // line), ([0] + near, z // line)):
+            first = side * line * tp
+            lines = pl.ds(pl.multiple_of(first * cap, 16), line * tp * cap)
             packed = jnp.dot(
                 placing_ref[hop, lines, :], state_ref[...], preferred_element_type=F32
             ).astype(BF16)
-            for i in range(tp):
+            for i in range(line * tp):
                 packed_ref[first + i] = packed[i * cap : (i + 1) * cap]
-            for c in range(tp):
-                if k or c:
-                    dispatch_copy(k, c).start()
-                else:
-                    arrived_ref[here, rows_of(0), :] = packed_ref[z * tp + t]
+            for k in blocks:
+                for c in cores:
+                    if k or c:
+                        dispatch_copy(k, c).start()
+        arrived_ref[here, rows_of(0), :] = packed_ref[z * tp + t]
 
     def forward(k):
         for c in cores:
@@ -193,6 +195,7 @@
                 dispatch_copy(k, c).wait_recv()
             for j in others:
                 forward_copy(k, c, j).start()
+        weigh(k, 0)
 
     def weigh(k, j):
         section = (s + sub - j) % sub
@@ -214,11 +217,9 @@
     def expand():
         dims = (((1,), (1,)), ((), ()))
         for j in range(sub):
-            if j:
-                for k in order:
-                    for c in cores:
-                        forward_copy(k, c, j).wait_recv()
-            for k in order:
+            for k in coming if j else ():
+                for c in cores:
+                    forward_copy(k, c, j).wait_recv()
                 weigh(k, j)
             section = (s + sub - j) % sub
             columns = pl.ds(pl.multiple_of(section * half, LANES), half)
@@ -280,11 +281,8 @@
     lax.fori_loop(0, turned_ref.shape[0] // tile, turn, 0)
 
     def one_hop(hop, carry):
-        forward(0)
-        forward(far[0])
-        for k, ahead in zip(near, far[1:]):
+        for k in coming:
             forward(k)
-            forward(ahead)
         expand()
         for c in cores:
             for j in others:

time: 154 us -> 153 us (level)
  no operation moved by 1% of the time
where the time goes in v7:
time: 153 us
  Pallas kernels  151 us (99%)
  local copies, waits for them, and re-layouts  1.67 us (1%)
    pallas_call x1, Pallas kernels, shards(): pl.pallas_call(functools.partial(chain_kernel, sizes), out_shape=jax.Shap...  151 us

profile of v7, /device:TPU:1, one launch (start us, length us, event | category | flops | bytes accessed | tf_op | source)
XLA Modules:
  0.0 152.9 jit_solution(12300187561078010618)
XLA Ops:
  0.0 151.2 %shard_map.64 = bf16[128,1024]{1,0:T(8,128)(2,1)} custom-call(bf16[128,1024]{1,0:T(8,128)(2,1)} %rows_hbm.1, s32[4,128]{1,0:T(4,128)} %bitcast.1, f32[1,4096]{1,0:T(1,128)} %gain_hbm.1, bf16[1,704,4096]{2,1,0:T(8,128)(2,1)} %gate_hbm.1, bf16[1,704,4096]{2,1,0:T(8,128)(2,1)} %up_hbm.1, bf16[1,704,4096]{2,1,0:T(8,128)(2,1)} %down_hbm.1), custom_call_target="tpu_custom_call" | custom-call | flops 8858370048 | bytes 17301504 | tf_op jit(solution)/shard_map/pallas_call | solution.py:335
  151.2 1.7 %copy.8 = bf16[128,1024]{1,0:T(8,128)(2,1)} copy(bf16[128,1024]{1,0:T(8,128)(2,1)} %shard_map.64) | data formatting | bytes 524288
